TPU v7x, 512 devices: a whole 4x8x8 slice. The times are simulated.
512 devices in a mesh: grp: 8 (over z_hi, x), gx: 8 (over z_lo, core), gy: 8 (over y).
Axes of the slice: x: 4, y: 8, z: 8 (z_hi: 2, z_lo: 4; z = z_hi * 4 + z_lo), core: 2. Of those that a mesh axis runs over, the one named last changes fastest.
Arguments:
- efield: float32 [8, 3, 128, 128, 128], P('grp', None, 'gx', 'gy'), may hold values from -6 to 6
- hfield: float32 [8, 3, 128, 128, 128], P('grp', None, 'gx', 'gy'), may hold values from -6 to 6
- fwd_dft: bfloat16 [8, 2, 2, 3, 128, 128, 128], P('grp', None, None, None, 'gx', 'gy'), may hold values from -6 to 6
- adj_dft: bfloat16 [8, 2, 2, 3, 128, 128, 128], P('grp', None, None, None, 'gx', 'gy'), may hold values from -6 to 6
- permittivity: float32 [128, 128, 128], P('gx', 'gy'), may hold values from 1 to 4
- source_amp: float32 [8, 128, 128], P('grp', 'gx', 'gy'), may hold values from -6 to 6
- source_plane: int32 [8], P('grp'), may hold values from 4 to 123
- freqs: float32 [8, 2], P('grp'), may hold values from 0.2 to 1.5
- pml_width: int32 [2], replicated, may hold values from 2 to 7
- design_blocks: int32 [128], replicated, may hold values from 0 to 255, as said below
Outputs:
- grad_step: float32 [2, 128, 128, 128], P(None, 'gx', 'gy')
Inputs may be any that keep to these rules, and one draw needn't show every extreme that they name: `design_blocks`: distinct block numbers.
All inputs are finite; a program needn't handle non-finite values.
Results may differ from a plain program's by a relative error of at most 0.0003.
Values sent between devices are 32-bit elements; how exact they have to be, the bound alone decides.
A program may use at most 64 MiB of HBM per device.

v0:
```python
import jax
import jax.numpy as jnp
from jax import lax
from jax.sharding import PartitionSpec as P

BS = 8
STEPS = 2
courant = 0.5
absorb = 0.8


def shifted(value, axis, steps):
    count = lax.axis_size(axis)
    leading, last = (max(0, -steps), min(count, count - steps))
    return lax.ppermute(value, axis, [(source, source + steps) for source in range(leading, last)])


def ahead_z(field):
    zero = jnp.zeros_like(field[:, :, :1])
    return jnp.concatenate([field[:, :, 1:], zero], 2) - field


def behind_z(field):
    zero = jnp.zeros_like(field[:, :, :1])
    return field - jnp.concatenate([zero, field[:, :, :-1]], 2)


def profile(cells, count, width):
    place = cells.astype(jnp.float32)
    dist = jnp.minimum(place, count - 1.0 - place)
    wide = width.astype(jnp.float32)
    return jnp.maximum(0.0, (wide - dist) / wide) ** 2


def update_magnetic(fields_e, fields_h, damp):
    ex, ey, ez = fields_e
    hx, hy, hz = fields_h
    rim_x = shifted(jnp.stack([ey[0], ez[0]]), "gx", -1)
    rim_y = shifted(jnp.stack([ex[:, 0], ez[:, 0]]), "gy", -1)
    ey_dx = jnp.concatenate([ey[1:], rim_x[0][None]], 0) - ey
    ez_dx = jnp.concatenate([ez[1:], rim_x[1][None]], 0) - ez
    ex_dy = jnp.concatenate([ex[:, 1:], rim_y[0][:, None]], 1) - ex
    ez_dy = jnp.concatenate([ez[:, 1:], rim_y[1][:, None]], 1) - ez
    hx = damp * (hx - courant * (ez_dy - ahead_z(ey)))
    hy = damp * (hy - courant * (ahead_z(ex) - ez_dx))
    hz = damp * (hz - courant * (ey_dx - ex_dy))
    return (hx, hy, hz)


def update_electric(fields_e, fields_h, damp, coef, drive):
    ex, ey, ez = fields_e
    hx, hy, hz = fields_h
    last_x = hx.shape[0] - 1
    last_y = hx.shape[1] - 1
    rim_x = shifted(jnp.stack([hy[last_x], hz[last_x]]), "gx", 1)
    rim_y = shifted(jnp.stack([hx[:, last_y], hz[:, last_y]]), "gy", 1)
    hy_dx = hy - jnp.concatenate([rim_x[0][None], hy[:-1]], 0)
    hz_dx = hz - jnp.concatenate([rim_x[1][None], hz[:-1]], 0)
    hx_dy = hx - jnp.concatenate([rim_y[0][:, None], hx[:, :-1]], 1)
    hz_dy = hz - jnp.concatenate([rim_y[1][:, None], hz[:, :-1]], 1)
    ex = damp * (ex + coef * (hz_dy - behind_z(hy)))
    ey = damp * (ey + coef * (behind_z(hx) - hz_dx))
    ez = damp * (ez + coef * (hy_dx - hx_dy) + drive)
    return (ex, ey, ez)


def body(
    efield,
    hfield,
    fwd_dft,
    adj_dft,
    permittivity,
    source_amp,
    source_plane,
    freqs,
    pml_width,
    design_blocks,
):
    cells_x, cells_y, cells_z = permittivity.shape
    total_x = cells_x * lax.axis_size("gx")
    total_y = cells_y * lax.axis_size("gy")
    global_x = lax.axis_index("gx") * cells_x + jnp.arange(cells_x, dtype=jnp.int32)
    global_y = lax.axis_index("gy") * cells_y + jnp.arange(cells_y, dtype=jnp.int32)
    plane = (jnp.arange(cells_z, dtype=jnp.int32) == source_plane[0]).astype(jnp.float32)
    shaped = source_amp[0][:, :, None] * plane[None, None, :]
    omega = freqs[0]
    acc = adj_dft[0].astype(jnp.float32)
    damp = jnp.exp(
        -absorb
        * (
            profile(global_x, total_x, pml_width[0])[:, None]
            + profile(global_y, total_y, pml_width[1])[None, :]
        )
    )[:, :, None]
    coef = courant / permittivity
    fields_e = (efield[0, 0], efield[0, 1], efield[0, 2])
    fields_h = (hfield[0, 0], hfield[0, 1], hfield[0, 2])
    for step in range(STEPS):
        tval = jnp.float32(step + 1)
        fields_h = update_magnetic(fields_e, fields_h, damp)
        fields_e = update_electric(
            fields_e, fields_h, damp, coef, shaped * jnp.sin(omega[0] * tval)
        )
        efull = jnp.stack(fields_e)
        cosv = jnp.cos(omega * tval)[:, None, None, None, None]
        sinv = jnp.sin(omega * tval)[:, None, None, None, None]
        acc = jnp.stack([acc[:, 0] + cosv * efull, acc[:, 1] - sinv * efull], axis=1)
    cell_id = (global_x // BS)[:, None] * (total_y // BS) + (global_y // BS)[None, :]
    mask = jnp.any(design_blocks[:, None, None] == cell_id[None], axis=0).astype(jnp.float32)[
        :, :, None
    ]
    term = jnp.sum(fwd_dft[0].astype(jnp.float32) * acc, axis=(1, 2)) * mask[None]
    count = jnp.float32(design_blocks.shape[0] * BS * BS * cells_z)
    grad = lax.psum(term, "grp")
    squares = lax.psum(jnp.sum(grad * grad, axis=(1, 2, 3)), ("gx", "gy"))
    return grad / jnp.sqrt(squares / count + 1e-05)[:, None, None, None]


def solution(mesh):
    in_specs = (
        P("grp", None, "gx", "gy", None),
        P("grp", None, "gx", "gy", None),
        P("grp", None, None, None, "gx", "gy", None),
        P("grp", None, None, None, "gx", "gy", None),
        P("gx", "gy", None),
        P("grp", "gx", "gy"),
        P("grp"),
        P("grp", None),
        P(),
        P(),
    )
    out_specs = P(None, "gx", "gy", None)
    return jax.shard_map(body, mesh=mesh, in_specs=in_specs, out_specs=out_specs, check_vma=False)
```

profile of v0, /device:TPU:8, one launch (start us, length us, event | category | flops | bytes accessed | tf_op | source)
XLA Modules:
  0.0 310.4 jit_solution(465055666218704547)
XLA Ops:
  6.5 0.0 copy-start.2
  6.5 0.0 all-reduce.10.cloned.1.call-start
  6.5 1.1 slice_bitcast_fusion.1
  7.7 0.0 copy-start.7
  7.7 7.7 %collective-permute-start.1 = (f32[2,16,128]{2,1,0:T(8,128)S(1)}, f32[2,16,128]{2,1,0:T(8,128)S(1)}, u32[]{:S(2)}, u32[]{:S(2)}) collective-permute-start(f32[2,16,128]{2,1,0:T(8,128)S(1)} %pad_maximum_fusion.3), channel_id=1, source_target_pairs={{1,0},{2,1},{3,2},{4,3},{5,4},{6,5},{7,6},{9,8},{10,9},{11,10},{12... | collective-permute-start | bytes 49160 | tf_op jit(solution)/shard_map/ppermute | solution.py:15
  15.5 0.7 slice_bitcast_fusion.6
  16.2 1.3 collective-permute-start
  17.5 1.0 slice_bitcast_fusion.4
  18.5 1.4 fusion.73
  21.9 0.7 cosine_bitcast_fusion.1
  22.6 0.0 copy-done.2
  22.6 0.0 copy-start.6
  22.6 0.0 copy-start
  22.6 0.0 copy-start.4
  22.6 0.1 bitcast_convert_fusion
  22.8 0.1 multiply_exponential_fusion
  22.9 0.1 broadcast_add_fusion
  23.0 0.0 copy-done.7
  23.0 0.4 compare_reduce_fusion
  23.5 0.1 slice.303
  23.6 0.1 slice.298
  23.7 0.0 copy-start.1
  23.7 0.0 copy-start.5
  23.7 0.0 copy-done.6
  23.9 0.0 collective-permute-done.1
  23.9 0.0 collective-permute-done
  24.0 0.0 copy-done
  24.0 0.0 copy-done.4
  24.0 0.1 fusion.15
  24.2 0.1 fusion.23
  24.3 3.0 collective-permute-start.3
  27.4 1.9 collective-permute-start.2
  29.3 0.0 collective-permute-done.3
  29.4 3.7 %collective-permute-done.2 = f32[2,16,128]{2,1,0:T(8,128)S(1)} collective-permute-done((f32[2,16,128]{2,1,0:T(8,128)S(1)}, f32[2,16,128]{2,1,0:T(8,128)S(1)}, u32[]{:S(2)}, u32[]{:S(2)}) %collective-permute-start.2) | collective-permute-done | bytes 16416 | tf_op jit(solution)/shard_map/ppermute | solution.py:15
  33.0 0.0 copy-done.1
  33.0 0.0 copy-done.5
  33.0 0.2 fusion.19
  33.3 0.1 fusion.27
  33.5 1.3 collective-permute-start.4
  34.8 0.1 slice.325
  35.0 0.1 slice.330
  35.1 1.9 collective-permute-start.5
  37.0 0.0 collective-permute-done.4
  37.0 3.7 %collective-permute-done.5 = f32[2,16,128]{2,1,0:T(8,128)S(1)} collective-permute-done((f32[2,16,128]{2,1,0:T(8,128)S(1)}, f32[2,16,128]{2,1,0:T(8,128)S(1)}, u32[]{:S(2)}, u32[]{:S(2)}) %collective-permute-start.5) | collective-permute-done | bytes 16416 | tf_op jit(solution)/shard_map/ppermute | solution.py:15
  40.7 0.2 fusion.38
  41.0 2.0 collective-permute-start.7
  43.1 1.9 collective-permute-start.6
  45.0 0.0 collective-permute-done.7
  45.0 0.1 fusion.52
  45.2 3.6 %collective-permute-done.6 = f32[2,16,128]{2,1,0:T(8,128)S(1)} collective-permute-done((f32[2,16,128]{2,1,0:T(8,128)S(1)}, f32[2,16,128]{2,1,0:T(8,128)S(1)}, u32[]{:S(2)}, u32[]{:S(2)}) %collective-permute-start.6) | collective-permute-done | bytes 16416 | tf_op jit(solution)/shard_map/ppermute | solution.py:15
  48.7 0.2 fusion.43
  49.0 0.0 copy-start.3
  49.0 0.3 fusion.2
  49.3 0.8 copy-done.3
  50.1 0.2 fusion
  50.3 0.8 broadcast_multiply_fusion
  51.1 0.0 all-reduce.10.cloned.1.call-update
  51.1 115.3 %all-reduce.10.cloned.1.call-done = f32[2,16,16,128]{3,2,1,0:T(8,128)} async-done(((f32[2,16,16,128]{3,2,1,0:T(8,128)}), f32[2,16,16,128]{3,2,1,0:T(8,128)}) %all-reduce.10.cloned.1.call-update) | async-done | bytes 262160 | tf_op jit(solution)/shard_map/psum | solution.py:114
  166.4 1.1 multiply_reduce_fusion
  167.5 134.2 %psum.15 = f32[2]{0:T(128)S(1)} all-reduce(f32[2]{0:T(128)S(1)} %multiply_reduce_fusion), channel_id=1, replica_groups=mesh['grp'=8,'gx'=8,'gy'=8] {'gx','gy'}, use_global_device_ids=true, to_apply=%region_4.5 | all-reduce | flops 2 | bytes 16 | tf_op jit(solution)/shard_map/psum | solution.py:115
  301.8 1.7 broadcast_divide_fusion
  (47 shorter events, 0.4 us)
Async XLA Ops:
  6.5 16.0 %copy-start.2 = (bf16[1,2,2,3,16,16,128]{6,5,4,3,2,1,0:T(8,128)(2,1)S(1)}, bf16[1,2,2,3,16,16,128]{6,5,4,3,2,1,0:T(8,128)(2,1)}, u32[]{:S(2)}) copy-start(bf16[1,2,2,3,16,16,128]{6,5,4,3,2,1,0:T(8,128)(2,1)} %param.13) | copy-start | bytes 2359300
  6.5 159.9 %all-reduce.10.cloned.1.call-start = ((), (), s32[]{:S(2)}) async-start(), calls=%async_computation | async-start | bytes 524288 | tf_op jit(solution)/shard_map/psum | solution.py:114
  7.7 15.3 %copy-start.7 = (s32[128]{0:T(128)S(1)}, s32[128]{0:T(128)}, u32[]{:S(2)}) copy-start(s32[128]{0:T(128)} %param.19) | copy-start | bytes 1540
  7.7 16.2 %collective-permute-start.1 = (f32[2,16,128]{2,1,0:T(8,128)S(1)}, f32[2,16,128]{2,1,0:T(8,128)S(1)}, u32[]{:S(2)}, u32[]{:S(2)}) collective-permute-start(f32[2,16,128]{2,1,0:T(8,128)S(1)} %pad_maximum_fusion.3), channel_id=1, source_target_pairs={{1,0},{2,1},{3,2},{4,3},{5,4},{6,5},{7,6},{9,8},{10,9},{11,10},{12... | collective-permute-start | bytes 49160 | tf_op jit(solution)/shard_map/ppermute | solution.py:15
  16.2 7.8 %collective-permute-start = (f32[2,16,128]{2,1,0:T(8,128)S(1)}, f32[2,16,128]{2,1,0:T(8,128)S(1)}, u32[]{:S(2)}, u32[]{:S(2)}) collective-permute-start(f32[2,16,128]{2,1,0:T(8,128)S(1)} %pad_maximum_fusion.2), channel_id=1, source_target_pairs={{8,0},{16,8},{24,16},{32,24},{40,32},{48,40},{56,48},{9,1},{17,9},... | collective-permute-start | bytes 49160 | tf_op jit(solution)/shard_map/ppermute | solution.py:15
  22.6 1.1 copy-start.6
  22.6 1.4 copy-start
  22.6 1.4 copy-start.4
  23.7 9.4 %copy-start.1 = (f32[16,16,128]{2,1,0:T(8,128)S(1)}, f32[16,16,128]{2,1,0:T(8,128)}, u32[]{:S(2)}) copy-start(f32[16,16,128]{2,1,0:T(8,128)} %param.14) | copy-start | bytes 393220
  23.7 9.4 %copy-start.5 = (f32[1,16,16]{2,1,0:T(8,128)S(1)}, f32[1,16,16]{2,1,0:T(8,128)}, u32[]{:S(2)}) copy-start(f32[1,16,16]{2,1,0:T(8,128)} %param.15) | copy-start | bytes 3076
  24.3 5.0 %collective-permute-start.3 = (f32[2,16,128]{2,1,0:T(8,128)S(1)}, f32[2,16,128]{2,1,0:T(8,128)S(1)}, u32[]{:S(2)}, u32[]{:S(2)}) collective-permute-start(f32[2,16,128]{2,1,0:T(8,128)S(1)} %pad_maximum_fusion.5), channel_id=1, source_target_pairs={{0,8},{8,16},{16,24},{24,32},{32,40},{40,48},{48,56},{1,9},{9,17},... | collective-permute-start | bytes 49160 | tf_op jit(solution)/shard_map/ppermute | solution.py:15
  27.4 5.6 %collective-permute-start.2 = (f32[2,16,128]{2,1,0:T(8,128)S(1)}, f32[2,16,128]{2,1,0:T(8,128)S(1)}, u32[]{:S(2)}, u32[]{:S(2)}) collective-permute-start(f32[2,16,128]{2,1,0:T(8,128)S(1)} %pad_maximum_fusion.4), channel_id=1, source_target_pairs={{0,1},{1,2},{2,3},{3,4},{4,5},{5,6},{6,7},{8,9},{9,10},{10,11},{11... | collective-permute-start | bytes 49160 | tf_op jit(solution)/shard_map/ppermute | solution.py:15
  33.5 3.6 %collective-permute-start.4 = (f32[2,16,128]{2,1,0:T(8,128)S(1)}, f32[2,16,128]{2,1,0:T(8,128)S(1)}, u32[]{:S(2)}, u32[]{:S(2)}) collective-permute-start(f32[2,16,128]{2,1,0:T(8,128)S(1)} %pad_maximum_fusion.6), channel_id=1, source_target_pairs={{8,0},{16,8},{24,16},{32,24},{40,32},{48,40},{56,48},{9,1},{17,9},... | collective-permute-start | bytes 49160 | tf_op jit(solution)/shard_map/ppermute | solution.py:15
  35.1 5.6 %collective-permute-start.5 = (f32[2,16,128]{2,1,0:T(8,128)S(1)}, f32[2,16,128]{2,1,0:T(8,128)S(1)}, u32[]{:S(2)}, u32[]{:S(2)}) collective-permute-start(f32[2,16,128]{2,1,0:T(8,128)S(1)} %pad_maximum_fusion.7), channel_id=1, source_target_pairs={{1,0},{2,1},{3,2},{4,3},{5,4},{6,5},{7,6},{9,8},{10,9},{11,10},{12... | collective-permute-start | bytes 49160 | tf_op jit(solution)/shard_map/ppermute | solution.py:15
  41.0 4.0 %collective-permute-start.7 = (f32[2,16,128]{2,1,0:T(8,128)S(1)}, f32[2,16,128]{2,1,0:T(8,128)S(1)}, u32[]{:S(2)}, u32[]{:S(2)}) collective-permute-start(f32[2,16,128]{2,1,0:T(8,128)S(1)} %pad_maximum_fusion.9), channel_id=1, source_target_pairs={{0,8},{8,16},{16,24},{24,32},{32,40},{40,48},{48,56},{1,9},{9,17},... | collective-permute-start | bytes 49160 | tf_op jit(solution)/shard_map/ppermute | solution.py:15
  43.1 5.7 %collective-permute-start.6 = (f32[2,16,128]{2,1,0:T(8,128)S(1)}, f32[2,16,128]{2,1,0:T(8,128)S(1)}, u32[]{:S(2)}, u32[]{:S(2)}) collective-permute-start(f32[2,16,128]{2,1,0:T(8,128)S(1)} %pad_maximum_fusion.8), channel_id=1, source_target_pairs={{0,1},{1,2},{2,3},{3,4},{4,5},{5,6},{6,7},{8,9},{9,10},{10,11},{11... | collective-permute-start | bytes 49160 | tf_op jit(solution)/shard_map/ppermute | solution.py:15
  49.0 1.1 copy-start.3
Sparse Core Ops, SparseCore 0:
  51.3 115.1 all-reduce.9
where the time goes:
time: 311 us; the launch traced here: 310 us
  blocking collectives  134 us (43%)
  waiting for transfers between devices  126 us (41%)
  starting transfers between devices  21.1 us (7%)
  between operations  16.2 us (5%)
  other arithmetic  6.79 us (2%)
  local copies, waits for them, and re-layouts  5.7 us (2%)
    psum x1, blocking collectives, body(): squares = lax.psum(jnp.sum(grad * grad, axis=(1, 2, 3)), ('gx', 'gy'))  134 us
    psum x1, waiting for transfers between devices, body(): grad = lax.psum(term, 'grp')  115 us
    ppermute x8, starting transfers between devices, shifted(): lax.ppermute(value, axis, [(source, source + steps) for source in range(l...  21.1 us
    ppermute x8, waiting for transfers between devices, shifted(): lax.ppermute(value, axis, [(source, source + steps) for source in range(l...  11 us
  transfers between devices with their start and end apart: 9, of which 4 were waited for; matrix products, arithmetic and copies ran while one was open for 2% of the time, Pallas kernels for 0%

commit v1 on v0

--- a/solution.py
+++ b/solution.py
@@ -111,7 +111,11 @@
     ]
     term = jnp.sum(fwd_dft[0].astype(jnp.float32) * acc, axis=(1, 2)) * mask[None]
     count = jnp.float32(design_blocks.shape[0] * BS * BS * cells_z)
-    grad = lax.psum(term, "grp")
+
+    def play_squares(message, a_name):
+        return jnp.sum(jax.lax.all_gather(message, a_name), 0)
+
+    grad = play_squares(term, "grp")
     squares = lax.psum(jnp.sum(grad * grad, axis=(1, 2, 3)), ("gx", "gy"))
     return grad / jnp.sqrt(squares / count + 1e-05)[:, None, None, None]
 

time: 311 us -> 281 us (0.904)
  the two profiles are of different devices: /device:TPU:8 before, /device:TPU:2 now
where the time goes in v1:
time: 281 us; the launch traced here: 280 us
  blocking collectives  135 us (48%)
  waiting for transfers between devices  97.8 us (35%)
  starting transfers between devices  18.9 us (7%)
  between operations  16.2 us (6%)
  other arithmetic  6.58 us (2%)
  local copies, waits for them, and re-layouts  5.7 us (2%)
    psum x1, blocking collectives, body(): squares = lax.psum(jnp.sum(grad * grad, axis=(1, 2, 3)), ('gx', 'gy'))  135 us
    all_gather x1, waiting for transfers between devices, play_squares(): return jnp.sum(jax.lax.all_gather(message, a_name), 0)  90.5 us
    ppermute x8, starting transfers between devices, shifted(): lax.ppermute(value, axis, [(source, source + steps) for source in range(l...  18.9 us
    ppermute x8, waiting for transfers between devices, shifted(): lax.ppermute(value, axis, [(source, source + steps) for source in range(l...  7.29 us
  transfers between devices with their start and end apart: 9, of which 5 were waited for; matrix products, arithmetic and copies ran while one was open for 2% of the time, Pallas kernels for 0%

profile of v1, /device:TPU:2, one launch (start us, length us, event | category | flops | bytes accessed | tf_op | source)
XLA Modules:
  0.0 280.0 jit_solution(8659843185707431241)
XLA Ops:
  6.5 0.0 copy-start.2
  6.5 0.0 all-gather.2.cloned.1.call-start
  6.5 1.1 slice_bitcast_fusion.1
  7.7 0.0 copy-start.7
  7.7 1.3 collective-permute-start.1
  9.0 0.7 slice_bitcast_fusion.6
  9.7 1.3 collective-permute-start
  11.0 1.0 slice_bitcast_fusion.4
  12.0 1.4 fusion.73
  15.4 0.7 cosine_bitcast_fusion.1
  16.1 0.0 copy-done.2
  16.1 0.0 copy-start.6
  16.1 0.0 copy-start
  16.2 0.0 copy-start.4
  16.2 0.1 bitcast_convert_fusion
  16.4 0.1 multiply_exponential_fusion
  16.4 0.1 broadcast_add_fusion
  16.5 0.0 copy-done.7
  16.5 0.4 compare_reduce_fusion
  17.0 0.1 slice.303
  17.1 0.1 slice.298
  17.2 0.0 copy-start.1
  17.2 0.0 copy-start.5
  17.2 0.0 copy-done.6
  17.5 0.0 collective-permute-done.1
  17.5 0.0 collective-permute-done
  17.5 0.0 copy-done
  17.5 0.0 copy-done.4
  17.5 0.1 fusion.15
  17.7 0.1 fusion.23
  17.8 3.0 %collective-permute-start.3 = (f32[2,16,128]{2,1,0:T(8,128)S(1)}, f32[2,16,128]{2,1,0:T(8,128)S(1)}, u32[]{:S(2)}, u32[]{:S(2)}) collective-permute-start(f32[2,16,128]{2,1,0:T(8,128)S(1)} %pad_maximum_fusion.5), channel_id=1, source_target_pairs={{0,8},{8,16},{16,24},{24,32},{32,40},{40,48},{48,56},{1,9},{9,17},... | collective-permute-start | bytes 49160 | tf_op jit(solution)/shard_map/ppermute | solution.py:15
  20.9 4.5 %collective-permute-start.2 = (f32[2,16,128]{2,1,0:T(8,128)S(1)}, f32[2,16,128]{2,1,0:T(8,128)S(1)}, u32[]{:S(2)}, u32[]{:S(2)}) collective-permute-start(f32[2,16,128]{2,1,0:T(8,128)S(1)} %pad_maximum_fusion.4), channel_id=1, source_target_pairs={{0,1},{1,2},{2,3},{3,4},{4,5},{5,6},{6,7},{8,9},{9,10},{10,11},{11... | collective-permute-start | bytes 49160 | tf_op jit(solution)/shard_map/ppermute | solution.py:15
  25.5 0.0 collective-permute-done.3
  25.5 1.4 collective-permute-done.2
  26.9 0.0 copy-done.1
  26.9 0.0 copy-done.5
  26.9 0.2 fusion.19
  27.2 0.1 fusion.27
  27.3 1.3 collective-permute-start.4
  28.7 0.1 slice.325
  28.8 0.1 slice.330
  29.0 1.3 collective-permute-start.5
  30.3 0.8 collective-permute-done.4
  31.0 3.8 %collective-permute-done.5 = f32[2,16,128]{2,1,0:T(8,128)S(1)} collective-permute-done((f32[2,16,128]{2,1,0:T(8,128)S(1)}, f32[2,16,128]{2,1,0:T(8,128)S(1)}, u32[]{:S(2)}, u32[]{:S(2)}) %collective-permute-start.5) | collective-permute-done | bytes 16416 | tf_op jit(solution)/shard_map/ppermute | solution.py:15
  34.9 0.1 fusion.38
  35.1 2.5 collective-permute-start.7
  37.7 3.6 %collective-permute-start.6 = (f32[2,16,128]{2,1,0:T(8,128)S(1)}, f32[2,16,128]{2,1,0:T(8,128)S(1)}, u32[]{:S(2)}, u32[]{:S(2)}) collective-permute-start(f32[2,16,128]{2,1,0:T(8,128)S(1)} %pad_maximum_fusion.8), channel_id=1, source_target_pairs={{0,1},{1,2},{2,3},{3,4},{4,5},{5,6},{6,7},{8,9},{9,10},{10,11},{11... | collective-permute-start | bytes 49160 | tf_op jit(solution)/shard_map/ppermute | solution.py:15
  41.3 0.0 collective-permute-done.7
  41.3 0.1 fusion.52
  41.5 1.3 collective-permute-done.6
  42.7 0.2 fusion.43
  43.0 0.0 copy-start.3
  43.0 0.3 fusion.2
  43.3 0.8 copy-done.3
  44.1 0.2 fusion
  44.3 0.8 bitcast_multiply_fusion
  45.1 0.0 all-gather.2.cloned.1.call-update
  45.1 90.5 %all-gather.2.cloned.1.call-done = f32[8,2,16,16,128]{4,3,2,1,0:T(8,128)} async-done(((f32[1,2,16,16,128]{4,3,2,1,0:T(8,128)}), f32[8,2,16,16,128]{4,3,2,1,0:T(8,128)}) %all-gather.2.cloned.1.call-update) | async-done | bytes 2097168 | tf_op jit(solution)/shard_map/all_gather | solution.py:116
  135.6 1.8 reduce_sum.31
  137.3 0.1 multiply_reduce_fusion
  137.5 134.9 %psum.7 = f32[2]{0:T(128)S(1)} all-reduce(f32[2]{0:T(128)S(1)} %multiply_reduce_fusion), channel_id=1, replica_groups=mesh['grp'=8,'gx'=8,'gy'=8] {'gx','gy'}, use_global_device_ids=true, to_apply=%region_4.5 | all-reduce | flops 2 | bytes 16 | tf_op jit(solution)/shard_map/psum | solution.py:119
  272.4 0.8 broadcast_divide_fusion
  (47 shorter events, 0.4 us)
Async XLA Ops:
  6.5 9.6 %copy-start.2 = (bf16[1,2,2,3,16,16,128]{6,5,4,3,2,1,0:T(8,128)(2,1)S(1)}, bf16[1,2,2,3,16,16,128]{6,5,4,3,2,1,0:T(8,128)(2,1)}, u32[]{:S(2)}) copy-start(bf16[1,2,2,3,16,16,128]{6,5,4,3,2,1,0:T(8,128)(2,1)} %param.13) | copy-start | bytes 2359300
  6.5 129.0 %all-gather.2.cloned.1.call-start = ((), (), s32[]{:S(2)}) async-start(), calls=%async_computation | async-start | bytes 2359296 | tf_op jit(solution)/shard_map/all_gather | solution.py:116
  7.7 8.9 %copy-start.7 = (s32[128]{0:T(128)S(1)}, s32[128]{0:T(128)}, u32[]{:S(2)}) copy-start(s32[128]{0:T(128)} %param.19) | copy-start | bytes 1540
  7.7 9.8 %collective-permute-start.1 = (f32[2,16,128]{2,1,0:T(8,128)S(1)}, f32[2,16,128]{2,1,0:T(8,128)S(1)}, u32[]{:S(2)}, u32[]{:S(2)}) collective-permute-start(f32[2,16,128]{2,1,0:T(8,128)S(1)} %pad_maximum_fusion.3), channel_id=1, source_target_pairs={{1,0},{2,1},{3,2},{4,3},{5,4},{6,5},{7,6},{9,8},{10,9},{11,10},{12... | collective-permute-start | bytes 49160 | tf_op jit(solution)/shard_map/ppermute | solution.py:15
  9.7 7.8 %collective-permute-start = (f32[2,16,128]{2,1,0:T(8,128)S(1)}, f32[2,16,128]{2,1,0:T(8,128)S(1)}, u32[]{:S(2)}, u32[]{:S(2)}) collective-permute-start(f32[2,16,128]{2,1,0:T(8,128)S(1)} %pad_maximum_fusion.2), channel_id=1, source_target_pairs={{8,0},{16,8},{24,16},{32,24},{40,32},{48,40},{56,48},{9,1},{17,9},... | collective-permute-start | bytes 49160 | tf_op jit(solution)/shard_map/ppermute | solution.py:15
  16.1 1.1 copy-start.6
  16.1 1.4 copy-start
  16.2 1.4 copy-start.4
  17.2 9.7 %copy-start.1 = (f32[16,16,128]{2,1,0:T(8,128)S(1)}, f32[16,16,128]{2,1,0:T(8,128)}, u32[]{:S(2)}) copy-start(f32[16,16,128]{2,1,0:T(8,128)} %param.14) | copy-start | bytes 393220
  17.2 9.7 %copy-start.5 = (f32[1,16,16]{2,1,0:T(8,128)S(1)}, f32[1,16,16]{2,1,0:T(8,128)}, u32[]{:S(2)}) copy-start(f32[1,16,16]{2,1,0:T(8,128)} %param.15) | copy-start | bytes 3076
  17.8 7.7 %collective-permute-start.3 = (f32[2,16,128]{2,1,0:T(8,128)S(1)}, f32[2,16,128]{2,1,0:T(8,128)S(1)}, u32[]{:S(2)}, u32[]{:S(2)}) collective-permute-start(f32[2,16,128]{2,1,0:T(8,128)S(1)} %pad_maximum_fusion.5), channel_id=1, source_target_pairs={{0,8},{8,16},{16,24},{24,32},{32,40},{40,48},{48,56},{1,9},{9,17},... | collective-permute-start | bytes 49160 | tf_op jit(solution)/shard_map/ppermute | solution.py:15
  20.9 6.0 %collective-permute-start.2 = (f32[2,16,128]{2,1,0:T(8,128)S(1)}, f32[2,16,128]{2,1,0:T(8,128)S(1)}, u32[]{:S(2)}, u32[]{:S(2)}) collective-permute-start(f32[2,16,128]{2,1,0:T(8,128)S(1)} %pad_maximum_fusion.4), channel_id=1, source_target_pairs={{0,1},{1,2},{2,3},{3,4},{4,5},{5,6},{6,7},{8,9},{9,10},{10,11},{11... | collective-permute-start | bytes 49160 | tf_op jit(solution)/shard_map/ppermute | solution.py:15
  27.3 3.7 %collective-permute-start.4 = (f32[2,16,128]{2,1,0:T(8,128)S(1)}, f32[2,16,128]{2,1,0:T(8,128)S(1)}, u32[]{:S(2)}, u32[]{:S(2)}) collective-permute-start(f32[2,16,128]{2,1,0:T(8,128)S(1)} %pad_maximum_fusion.6), channel_id=1, source_target_pairs={{8,0},{16,8},{24,16},{32,24},{40,32},{48,40},{56,48},{9,1},{17,9},... | collective-permute-start | bytes 49160 | tf_op jit(solution)/shard_map/ppermute | solution.py:15
  29.0 5.9 %collective-permute-start.5 = (f32[2,16,128]{2,1,0:T(8,128)S(1)}, f32[2,16,128]{2,1,0:T(8,128)S(1)}, u32[]{:S(2)}, u32[]{:S(2)}) collective-permute-start(f32[2,16,128]{2,1,0:T(8,128)S(1)} %pad_maximum_fusion.7), channel_id=1, source_target_pairs={{1,0},{2,1},{3,2},{4,3},{5,4},{6,5},{7,6},{9,8},{10,9},{11,10},{12... | collective-permute-start | bytes 49160 | tf_op jit(solution)/shard_map/ppermute | solution.py:15
  35.1 6.2 %collective-permute-start.7 = (f32[2,16,128]{2,1,0:T(8,128)S(1)}, f32[2,16,128]{2,1,0:T(8,128)S(1)}, u32[]{:S(2)}, u32[]{:S(2)}) collective-permute-start(f32[2,16,128]{2,1,0:T(8,128)S(1)} %pad_maximum_fusion.9), channel_id=1, source_target_pairs={{0,8},{8,16},{16,24},{24,32},{32,40},{40,48},{48,56},{1,9},{9,17},... | collective-permute-start | bytes 49160 | tf_op jit(solution)/shard_map/ppermute | solution.py:15
  37.7 5.1 %collective-permute-start.6 = (f32[2,16,128]{2,1,0:T(8,128)S(1)}, f32[2,16,128]{2,1,0:T(8,128)S(1)}, u32[]{:S(2)}, u32[]{:S(2)}) collective-permute-start(f32[2,16,128]{2,1,0:T(8,128)S(1)} %pad_maximum_fusion.8), channel_id=1, source_target_pairs={{0,1},{1,2},{2,3},{3,4},{4,5},{5,6},{6,7},{8,9},{9,10},{10,11},{11... | collective-permute-start | bytes 49160 | tf_op jit(solution)/shard_map/ppermute | solution.py:15
  43.0 1.1 copy-start.3
Sparse Core Ops, SparseCore 0:
  45.2 90.2 all-gather.1
